TPU v7x, 32 devices: a whole 2x2x4 slice. The times are simulated.
32 devices in a mesh: groups: 2 (over y), space: 4 (over z), tm: 2 (over x), obs: 2 (over core).
Axes of the slice: x: 2, y: 2, z: 4, core: 2. Of those that a mesh axis runs over, the one named last changes fastest.
Arguments:
- footprint: bfloat16 [4, 4, 4, 256, 256], P('space', ('tm', 'obs')), may hold values from -0.1875 to 0.1875
- tile_index: int32 [8, 4, 4], P(('groups', 'space'), ('tm', 'obs')), parts along dimension 0, may hold values from 0 to 1
- assign: int32 [8, 4], P(('groups', 'tm', 'obs')), parts along dimension 0, may hold values from 0 to 3, each once within a row
- land: int32 [4], P('space'), may hold values 0 or 1
- sigma: float32 [16, 128], P(('groups', 'space')), parts along dimension 0, may hold values from 0.3 to 1.5
- departures: float32 [8, 4, 256, 128], P(('groups', 'tm', 'obs'), 'space'), parts along dimension 0, may hold values from -6 to 6
- rinv: float32 [8, 4, 256], P(('groups', 'tm', 'obs'), 'space'), parts along dimension 0, may hold values from 0.25 to 2
- alpha: float32 [4, 128], P('groups'), parts along dimension 0, may hold values from 0.1 to 0.4
- beta: float32 [2, 128], P('groups'), parts along dimension 0, may hold values from 0.2 to 0.8
Outputs:
- increment: float32 [8, 8, 128, 128], P(('groups', 'tm'), 'space'), parts along dimension 0
- weighted: float32 [8, 4, 256, 128], P(('groups', 'tm', 'obs'), 'space'), parts along dimension 0
There are 2 independent parts, one for each index of `groups`. A program takes and returns all parts, laid end to end along the dimension named above; an argument that names none is the same for every part. Nothing has to cross between parts.
Inputs may be any that keep to these rules, and one draw needn't show every extreme that they name: `assign`: each row holds every block number once.
All inputs are finite; a program needn't handle non-finite values. No bound on the sum of `land` on one device may be relied on, other than what follows from the above.
Results may differ from a plain program's by a relative error of at most 0.017.
Values may be sent and summed in bfloat16 or wider, within the bound.
A program may use at most 64 MiB of HBM per device.

v0:
```python
import jax
import jax.numpy as jnp
from jax import lax
from jax.sharding import PartitionSpec as P

TW = 2
ITERS = 2


OCEAN = 0.35
SPATIAL = 0.2
TEMPORAL = 0.6


def as_sent(shard):
    return jax.tree.map(lambda a: a.astype(jnp.bfloat16) if a.dtype == jnp.float32 else a, shard)


def padded_2(block, sides, width):
    for axis, dim in sides:
        count = lax.axis_size(axis)
        forward = [(i, i + 1) for i in range(count - 1)]
        backward = [(target, source) for source, target in forward]
        low = lax.ppermute(
            lax.slice_in_dim(block, block.shape[dim] - width, None, axis=dim), axis, forward
        )
        high = lax.ppermute(lax.slice_in_dim(block, 0, width, axis=dim), axis, backward)
        block = jnp.concatenate([low, block, high], axis=dim)
    return block


def from_behind(block, axis, distance):
    devices = range(lax.axis_size(axis))
    route = [(i - distance, i) for i in devices if i - distance in devices]
    return lax.ppermute(block, axis, route)


def shards(footprint, tile_index, assign, land, sigma, departures, rinv, alpha, beta):
    tiles = footprint[0, 0]
    which = tile_index[0, 0]
    order = assign[0]
    weights = rinv[0][:, :, None]
    observed = departures[0]
    per_row = sigma.shape[0] // land.shape[0]
    scale_rows = jnp.repeat(jnp.where(land == 1, 1.0, OCEAN).astype(jnp.float32), per_row)
    spread = (sigma * scale_rows[:, None])[None, :, :, None]
    members = alpha.shape[1]
    width = tiles.shape[1]
    count = TW * sigma.shape[0] * sigma.shape[1] // width
    field_shape = (TW, sigma.shape[0], sigma.shape[1], members)
    back = jnp.argsort(order)
    picks = (which[None, :] == jnp.arange(count)[:, None]).astype(jnp.float32)

    def smooth_rows(field):
        padded = padded_2(as_sent(field), (("space", 1),), 1).astype(field.dtype)
        across = jnp.pad(field[:, :, 1:], ((0, 0), (0, 0), (0, 1), (0, 0)))
        across = across + jnp.pad(field[:, :, :-1], ((0, 0), (0, 0), (1, 0), (0, 0)))
        return field + SPATIAL * (padded[:, 2:] + padded[:, :-2] + across)

    def correlate(field):
        earlier = from_behind(as_sent(field[-1:]), "tm", 1)
        before = jnp.concatenate([earlier, field[:-1]], axis=0)
        return spread * smooth_rows(field + TEMPORAL * before)

    def correlate_adjoint(field):
        smoothed = smooth_rows(spread * field)
        later = from_behind(smoothed[:1].astype(jnp.bfloat16), "tm", -1).astype(jnp.float32)
        after = jnp.concatenate([smoothed[1:], later], axis=0)
        return smoothed + TEMPORAL * after

    def as_tiles(field):
        return field.astype(jnp.bfloat16).reshape(count, width, members)

    def partial_term(cells):
        picked = jnp.take(tiles, order, axis=0)
        inputs = jnp.take(cells, jnp.take(which, order), axis=0)
        return jnp.einsum("bij,bjm->bim", picked, inputs, preferred_element_type=jnp.float32)

    def observe(cells):
        return lax.psum_scatter(
            partial_term(cells).astype(jnp.bfloat16), "space", scatter_dimension=0, tiled=True
        ).astype(jnp.float32)

    def spread_owned(values):
        return lax.all_gather(values.astype(jnp.bfloat16), "space", axis=0, tiled=True)

    def adjoint(rounded_all):
        by_block = jnp.take(rounded_all, back, axis=0)
        contrib = jnp.einsum("bji,bjm->bim", tiles, by_block, preferred_element_type=jnp.float32)
        local = jnp.einsum("tb,bim->tim", picks, contrib, precision=lax.Precision.HIGHEST)
        total = lax.psum(local.astype(jnp.bfloat16), "obs").astype(jnp.float32)
        return correlate_adjoint(total.reshape(field_shape))

    gradient = adjoint(spread_owned(weights * observed))
    state = jnp.zeros(field_shape, jnp.float32)
    residual = gradient
    direction = gradient
    for step in range(ITERS):
        image_cells = as_tiles(correlate(direction))
        rounded = spread_owned(weights * observe(image_cells))
        image = direction + adjoint(rounded)
        state = state + alpha[step] * direction
        if step + 1 < ITERS:
            residual = residual - alpha[step] * image
            direction = residual + beta[step] * direction
    increment = correlate(state)
    fitted = observe(as_tiles(increment))
    weighted = weights * (fitted - observed)
    return (increment, weighted[None])


def solution(mesh):
    in_specs = (
        P("space", ("tm", "obs"), None, None, None),
        P(("groups", "space"), ("tm", "obs"), None),
        P(("groups", "tm", "obs"), None),
        P("space"),
        P(("groups", "space"), None),
        P(("groups", "tm", "obs"), "space", None, None),
        P(("groups", "tm", "obs"), "space", None),
        P("groups", None),
        P("groups", None),
    )
    out_specs = (
        P(("groups", "tm"), "space", None, None),
        P(("groups", "tm", "obs"), "space", None, None),
    )
    return jax.shard_map(shards, mesh=mesh, in_specs=in_specs, out_specs=out_specs, check_vma=False)
```

profile of v0, /device:TPU:0, one launch (start us, length us, event | category | flops | bytes accessed | tf_op | source)
XLA Modules:
  0.0 199.9 jit_solution(12974666108348094286)
XLA Ops:
  10.4 15.6 %all_gather.6 = bf16[4,256,128]{2,1,0:T(8,128)(2,1)S(1)} all-gather(bf16[1,256,128]{2,1,0:T(8,128)(2,1)S(1)} %fusion.33), channel_id=1, replica_groups=mesh['groups'=2,'space'=4,'tm'=2,'obs'=2] {'space'}, dimensions={0}, use_global_device_ids=true | all-gather | bytes 327680 | tf_op jit(solution)/shard_map/all_gather | solution.py:85
  31.2 17.6 %all-reduce.11.cloned.1.call-done = bf16[2,2,128,128]{3,2,1,0:T(8,128)(2,1)} async-done(((bf16[2,2,128,128]{3,2,1,0:T(8,128)(2,1)}), bf16[2,2,128,128]{3,2,1,0:T(8,128)(2,1)}) %all-reduce.11.cloned.1.call-update) | async-done | bytes 131088 | tf_op jit(solution)/shard_map/psum | solution.py:91
  48.8 1.0 convert_multiply_fusion.1
  49.8 3.6 %collective-permute-start = (bf16[2,1,128,128]{3,2,1,0:T(8,128)(2,1)S(1)}, bf16[2,1,128,128]{3,2,1,0:T(8,128)(2,1)S(1)}, u32[]{:S(2)}, u32[]{:S(2)}) collective-permute-start(bf16[2,1,128,128]{3,2,1,0:T(8,128)(2,1)S(1)} %get-tuple-element.35), channel_id=1, source_target_pairs={{0,4},{4,8},{8,12},{1,5},{5,9},{9,13},{2,6},{6,10},{10,14},{3,7},{... | collective-permute-start | bytes 196616 | tf_op jit(solution)/shard_map/ppermute | solution.py:24
  53.5 1.3 collective-permute-start.1
  55.4 4.3 %collective-permute-done.1 = bf16[2,1,128,128]{3,2,1,0:T(8,128)(2,1)S(1)} collective-permute-done((bf16[2,1,128,128]{3,2,1,0:T(8,128)(2,1)S(1)}, bf16[2,1,128,128]{3,2,1,0:T(8,128)(2,1)S(1)}, u32[]{:S(2)}, u32[]{:S(2)}) %collective-permute-start.1) | collective-permute-done | bytes 65568 | tf_op jit(solution)/shard_map/ppermute | solution.py:27
  59.8 1.3 collective-permute-start.2
  61.7 4.2 %collective-permute-done.2 = bf16[1,2,128,128]{3,2,1,0:T(8,128)(2,1)S(1)} collective-permute-done((bf16[1,2,128,128]{3,2,1,0:T(8,128)(2,1)S(1)}, bf16[1,2,128,128]{3,2,1,0:T(8,128)(2,1)S(1)}, u32[]{:S(2)}, u32[]{:S(2)}) %collective-permute-start.2) | collective-permute-done | bytes 65568 | tf_op jit(solution)/shard_map/ppermute | solution.py:35
  66.1 1.6 collective-permute-start.3
  67.7 1.9 collective-permute-done.3
  70.5 3.4 %collective-permute-start.4 = (bf16[2,1,128,128]{3,2,1,0:T(8,128)(2,1)S(1)}, bf16[2,1,128,128]{3,2,1,0:T(8,128)(2,1)S(1)}, u32[]{:S(2)}, u32[]{:S(2)}) collective-permute-start(bf16[2,1,128,128]{3,2,1,0:T(8,128)(2,1)S(1)} %get-tuple-element.33), channel_id=1, source_target_pairs={{0,4},{4,8},{8,12},{1,5},{5,9},{9,13},{2,6},{6,10},{10,14},{3,7},{... | collective-permute-start | bytes 196616 | tf_op jit(solution)/shard_map/ppermute | solution.py:24
  73.9 1.3 collective-permute-start.5
  75.8 4.3 %collective-permute-done.5 = bf16[2,1,128,128]{3,2,1,0:T(8,128)(2,1)S(1)} collective-permute-done((bf16[2,1,128,128]{3,2,1,0:T(8,128)(2,1)S(1)}, bf16[2,1,128,128]{3,2,1,0:T(8,128)(2,1)S(1)}, u32[]{:S(2)}, u32[]{:S(2)}) %collective-permute-start.5) | collective-permute-done | bytes 65568 | tf_op jit(solution)/shard_map/ppermute | solution.py:27
  80.9 1.1 convolution_convert_fusion.1
  82.0 19.7 %reduce-scatter.3.cloned.1.call-done = bf16[1,256,128]{2,1,0:T(8,128)(2,1)} async-done(((bf16[4,256,128]{2,1,0:T(8,128)(2,1)}), bf16[1,256,128]{2,1,0:T(8,128)(2,1)}) %reduce-scatter.3.cloned.1.call-update) | async-done | bytes 65552 | tf_op jit(solution)/shard_map/reduce_scatter | solution.py:80
  102.7 13.9 %all_gather.7 = bf16[4,256,128]{2,1,0:T(8,128)(2,1)S(1)} all-gather(bf16[1,256,128]{2,1,0:T(8,128)(2,1)S(1)} %multiply_convert_fusion), channel_id=1, replica_groups=mesh['groups'=2,'space'=4,'tm'=2,'obs'=2] {'space'}, dimensions={0}, use_global_device_ids=true | all-gather | bytes 327680 | tf_op jit(solution)/shard_map/all_gather | solution.py:85
  119.1 16.2 %all-reduce.13.cloned.1.call-done = bf16[2,2,128,128]{3,2,1,0:T(8,128)(2,1)} async-done(((bf16[2,2,128,128]{3,2,1,0:T(8,128)(2,1)}), bf16[2,2,128,128]{3,2,1,0:T(8,128)(2,1)}) %all-reduce.13.cloned.1.call-update) | async-done | bytes 131088 | tf_op jit(solution)/shard_map/psum | solution.py:91
  135.3 1.0 convert_multiply_fusion
  136.3 3.6 %collective-permute-start.6 = (bf16[2,1,128,128]{3,2,1,0:T(8,128)(2,1)S(1)}, bf16[2,1,128,128]{3,2,1,0:T(8,128)(2,1)S(1)}, u32[]{:S(2)}, u32[]{:S(2)}) collective-permute-start(bf16[2,1,128,128]{3,2,1,0:T(8,128)(2,1)S(1)} %get-tuple-element.31), channel_id=1, source_target_pairs={{0,4},{4,8},{8,12},{1,5},{5,9},{9,13},{2,6},{6,10},{10,14},{3,7},{... | collective-permute-start | bytes 196616 | tf_op jit(solution)/shard_map/ppermute | solution.py:24
  140.0 1.3 collective-permute-start.7
  141.9 4.3 %collective-permute-done.7 = bf16[2,1,128,128]{3,2,1,0:T(8,128)(2,1)S(1)} collective-permute-done((bf16[2,1,128,128]{3,2,1,0:T(8,128)(2,1)S(1)}, bf16[2,1,128,128]{3,2,1,0:T(8,128)(2,1)S(1)}, u32[]{:S(2)}, u32[]{:S(2)}) %collective-permute-start.7) | collective-permute-done | bytes 65568 | tf_op jit(solution)/shard_map/ppermute | solution.py:27
  146.3 1.3 collective-permute-start.8
  147.7 4.8 %collective-permute-done.8 = bf16[1,2,128,128]{3,2,1,0:T(8,128)(2,1)S(1)} collective-permute-done((bf16[1,2,128,128]{3,2,1,0:T(8,128)(2,1)S(1)}, bf16[1,2,128,128]{3,2,1,0:T(8,128)(2,1)S(1)}, u32[]{:S(2)}, u32[]{:S(2)}) %collective-permute-start.8) | collective-permute-done | bytes 65568 | tf_op jit(solution)/shard_map/ppermute | solution.py:35
  153.4 1.1 fusion.23
  154.5 1.6 collective-permute-start.9
  156.1 1.9 collective-permute-done.9
  159.9 3.4 %collective-permute-start.10 = (bf16[2,1,128,128]{3,2,1,0:T(8,128)(2,1)S(1)}, bf16[2,1,128,128]{3,2,1,0:T(8,128)(2,1)S(1)}, u32[]{:S(2)}, u32[]{:S(2)}) collective-permute-start(bf16[2,1,128,128]{3,2,1,0:T(8,128)(2,1)S(1)} %get-tuple-element.29), channel_id=1, source_target_pairs={{0,4},{4,8},{8,12},{1,5},{5,9},{9,13},{2,6},{6,10},{10,14},{3,7},{... | collective-permute-start | bytes 196616 | tf_op jit(solution)/shard_map/ppermute | solution.py:24
  163.3 1.3 collective-permute-start.11
  165.2 4.3 %collective-permute-done.11 = bf16[2,1,128,128]{3,2,1,0:T(8,128)(2,1)S(1)} collective-permute-done((bf16[2,1,128,128]{3,2,1,0:T(8,128)(2,1)S(1)}, bf16[2,1,128,128]{3,2,1,0:T(8,128)(2,1)S(1)}, u32[]{:S(2)}, u32[]{:S(2)}) %collective-permute-start.11) | collective-permute-done | bytes 65568 | tf_op jit(solution)/shard_map/ppermute | solution.py:27
  170.9 1.1 convolution_convert_fusion
  172.0 19.8 %reduce-scatter.5.cloned.1.call-done = bf16[1,256,128]{2,1,0:T(8,128)(2,1)} async-done(((bf16[4,256,128]{2,1,0:T(8,128)(2,1)}), bf16[1,256,128]{2,1,0:T(8,128)(2,1)}) %reduce-scatter.5.cloned.1.call-update) | async-done | bytes 65552 | tf_op jit(solution)/shard_map/reduce_scatter | solution.py:80
  191.8 1.6 fusion.35
  (99 shorter events, 20.5 us)
Async XLA Ops:
  7.2 19.5 %copy-start = (bf16[1,1,4,256,256]{4,3,2,1,0:T(8,128)(2,1)S(1)}, bf16[1,1,4,256,256]{4,3,2,1,0:T(8,128)(2,1)}, u32[]{:S(2)}) copy-start(bf16[1,1,4,256,256]{4,3,2,1,0:T(8,128)(2,1)} %param.17) | copy-start | bytes 1572868
  7.2 41.6 %all-reduce.11.cloned.1.call-start = ((), (), s32[]{:S(2)}) async-start(), calls=%async_computation.2 | async-start | bytes 262144 | tf_op jit(solution)/shard_map/psum | solution.py:91
  7.2 0.7 copy-start.12
  8.7 0.7 copy-start.8
  27.2 0.7 copy-start.1
  29.2 72.6 %reduce-scatter.3.cloned.1.call-start = ((), (), s32[]{:S(2)}) async-start(), calls=%async_computation.3 | async-start | bytes 327680 | tf_op jit(solution)/shard_map/reduce_scatter | solution.py:80
  30.5 0.7 copy-start.9
  49.8 5.5 %collective-permute-start = (bf16[2,1,128,128]{3,2,1,0:T(8,128)(2,1)S(1)}, bf16[2,1,128,128]{3,2,1,0:T(8,128)(2,1)S(1)}, u32[]{:S(2)}, u32[]{:S(2)}) collective-permute-start(bf16[2,1,128,128]{3,2,1,0:T(8,128)(2,1)S(1)} %get-tuple-element.35), channel_id=1, source_target_pairs={{0,4},{4,8},{8,12},{1,5},{5,9},{9,13},{2,6},{6,10},{10,14},{3,7},{... | collective-permute-start | bytes 196616 | tf_op jit(solution)/shard_map/ppermute | solution.py:24
  53.5 6.2 %collective-permute-start.1 = (bf16[2,1,128,128]{3,2,1,0:T(8,128)(2,1)S(1)}, bf16[2,1,128,128]{3,2,1,0:T(8,128)(2,1)S(1)}, u32[]{:S(2)}, u32[]{:S(2)}) collective-permute-start(bf16[2,1,128,128]{3,2,1,0:T(8,128)(2,1)S(1)} %get-tuple-element.36), channel_id=1, source_target_pairs={{4,0},{8,4},{12,8},{5,1},{9,5},{13,9},{6,2},{10,6},{14,10},{7,3},{... | collective-permute-start | bytes 196616 | tf_op jit(solution)/shard_map/ppermute | solution.py:27
  54.8 4.9 %copy-start.6 = (bf16[2,2,128,128]{3,2,1,0:T(8,128)(2,1)S(1)}, bf16[2,2,128,128]{3,2,1,0:T(8,128)(2,1)}, u32[]{:S(2)}) copy-start(bf16[2,2,128,128]{3,2,1,0:T(8,128)(2,1)} %all-reduce.11.cloned.1.call-done) | copy-start | bytes 393220
  59.8 6.2 %collective-permute-start.2 = (bf16[1,2,128,128]{3,2,1,0:T(8,128)(2,1)S(1)}, bf16[1,2,128,128]{3,2,1,0:T(8,128)(2,1)S(1)}, u32[]{:S(2)}, u32[]{:S(2)}) collective-permute-start(bf16[1,2,128,128]{3,2,1,0:T(8,128)(2,1)S(1)} %slice.232), channel_id=1, source_target_pairs={{2,0},{3,1},{6,4},{7,5},{10,8},{11,9},{14,12},{15,13},{18,16},{19,... | collective-permute-start | bytes 196616 | tf_op jit(solution)/shard_map/ppermute | solution.py:35
  66.0 1.6 copy-start.4
  66.1 3.5 %collective-permute-start.3 = (bf16[1,2,128,128]{3,2,1,0:T(8,128)(2,1)S(1)}, bf16[1,2,128,128]{3,2,1,0:T(8,128)(2,1)S(1)}, u32[]{:S(2)}, u32[]{:S(2)}) collective-permute-start(bf16[1,2,128,128]{3,2,1,0:T(8,128)(2,1)S(1)} %slice.231), channel_id=1, source_target_pairs={{0,2},{1,3},{4,6},{5,7},{8,10},{9,11},{12,14},{13,15},{16,18},{17,... | collective-permute-start | bytes 196616 | tf_op jit(solution)/shard_map/ppermute | solution.py:35
  69.5 0.9 slice-start.2
  70.5 5.3 %collective-permute-start.4 = (bf16[2,1,128,128]{3,2,1,0:T(8,128)(2,1)S(1)}, bf16[2,1,128,128]{3,2,1,0:T(8,128)(2,1)S(1)}, u32[]{:S(2)}, u32[]{:S(2)}) collective-permute-start(bf16[2,1,128,128]{3,2,1,0:T(8,128)(2,1)S(1)} %get-tuple-element.33), channel_id=1, source_target_pairs={{0,4},{4,8},{8,12},{1,5},{5,9},{9,13},{2,6},{6,10},{10,14},{3,7},{... | collective-permute-start | bytes 196616 | tf_op jit(solution)/shard_map/ppermute | solution.py:24
  73.9 6.2 %collective-permute-start.5 = (bf16[2,1,128,128]{3,2,1,0:T(8,128)(2,1)S(1)}, bf16[2,1,128,128]{3,2,1,0:T(8,128)(2,1)S(1)}, u32[]{:S(2)}, u32[]{:S(2)}) collective-permute-start(bf16[2,1,128,128]{3,2,1,0:T(8,128)(2,1)S(1)} %get-tuple-element.34), channel_id=1, source_target_pairs={{4,0},{8,4},{12,8},{5,1},{9,5},{13,9},{6,2},{10,6},{14,10},{7,3},{... | collective-permute-start | bytes 196616 | tf_op jit(solution)/shard_map/ppermute | solution.py:27
  82.0 53.3 %all-reduce.13.cloned.1.call-start = ((), (), s32[]{:S(2)}) async-start(), calls=%async_computation.4 | async-start | bytes 262144 | tf_op jit(solution)/shard_map/psum | solution.py:91
  119.1 72.7 %reduce-scatter.5.cloned.1.call-start = ((), (), s32[]{:S(2)}) async-start(), calls=%async_computation.5 | async-start | bytes 327680 | tf_op jit(solution)/shard_map/reduce_scatter | solution.py:80
  136.3 5.5 %collective-permute-start.6 = (bf16[2,1,128,128]{3,2,1,0:T(8,128)(2,1)S(1)}, bf16[2,1,128,128]{3,2,1,0:T(8,128)(2,1)S(1)}, u32[]{:S(2)}, u32[]{:S(2)}) collective-permute-start(bf16[2,1,128,128]{3,2,1,0:T(8,128)(2,1)S(1)} %get-tuple-element.31), channel_id=1, source_target_pairs={{0,4},{4,8},{8,12},{1,5},{5,9},{9,13},{2,6},{6,10},{10,14},{3,7},{... | collective-permute-start | bytes 196616 | tf_op jit(solution)/shard_map/ppermute | solution.py:24
  140.0 6.2 %collective-permute-start.7 = (bf16[2,1,128,128]{3,2,1,0:T(8,128)(2,1)S(1)}, bf16[2,1,128,128]{3,2,1,0:T(8,128)(2,1)S(1)}, u32[]{:S(2)}, u32[]{:S(2)}) collective-permute-start(bf16[2,1,128,128]{3,2,1,0:T(8,128)(2,1)S(1)} %get-tuple-element.32), channel_id=1, source_target_pairs={{4,0},{8,4},{12,8},{5,1},{9,5},{13,9},{6,2},{10,6},{14,10},{7,3},{... | collective-permute-start | bytes 196616 | tf_op jit(solution)/shard_map/ppermute | solution.py:27
  141.3 4.9 %copy-start.7 = (bf16[2,2,128,128]{3,2,1,0:T(8,128)(2,1)S(1)}, bf16[2,2,128,128]{3,2,1,0:T(8,128)(2,1)}, u32[]{:S(2)}) copy-start(bf16[2,2,128,128]{3,2,1,0:T(8,128)(2,1)} %all-reduce.13.cloned.1.call-done) | copy-start | bytes 393220
  146.3 1.4 copy-start.3
  146.3 1.3 copy-start.10
  146.3 6.2 %collective-permute-start.8 = (bf16[1,2,128,128]{3,2,1,0:T(8,128)(2,1)S(1)}, bf16[1,2,128,128]{3,2,1,0:T(8,128)(2,1)S(1)}, u32[]{:S(2)}, u32[]{:S(2)}) collective-permute-start(bf16[1,2,128,128]{3,2,1,0:T(8,128)(2,1)S(1)} %slice.230), channel_id=1, source_target_pairs={{2,0},{3,1},{6,4},{7,5},{10,8},{11,9},{14,12},{15,13},{18,16},{19,... | collective-permute-start | bytes 196616 | tf_op jit(solution)/shard_map/ppermute | solution.py:35
  152.5 0.9 slice-start.1
  152.5 0.9 copy-start.11
  154.5 1.6 copy-start.2
  154.5 3.5 %collective-permute-start.9 = (bf16[1,2,128,128]{3,2,1,0:T(8,128)(2,1)S(1)}, bf16[1,2,128,128]{3,2,1,0:T(8,128)(2,1)S(1)}, u32[]{:S(2)}, u32[]{:S(2)}) collective-permute-start(bf16[1,2,128,128]{3,2,1,0:T(8,128)(2,1)S(1)} %slice.229), channel_id=1, source_target_pairs={{0,2},{1,3},{4,6},{5,7},{8,10},{9,11},{12,14},{13,15},{16,18},{17,... | collective-permute-start | bytes 196616 | tf_op jit(solution)/shard_map/ppermute | solution.py:35
  158.0 0.9 slice-start
  159.9 5.3 %collective-permute-start.10 = (bf16[2,1,128,128]{3,2,1,0:T(8,128)(2,1)S(1)}, bf16[2,1,128,128]{3,2,1,0:T(8,128)(2,1)S(1)}, u32[]{:S(2)}, u32[]{:S(2)}) collective-permute-start(bf16[2,1,128,128]{3,2,1,0:T(8,128)(2,1)S(1)} %get-tuple-element.29), channel_id=1, source_target_pairs={{0,4},{4,8},{8,12},{1,5},{5,9},{9,13},{2,6},{6,10},{10,14},{3,7},{... | collective-permute-start | bytes 196616 | tf_op jit(solution)/shard_map/ppermute | solution.py:24
  163.3 6.2 %collective-permute-start.11 = (bf16[2,1,128,128]{3,2,1,0:T(8,128)(2,1)S(1)}, bf16[2,1,128,128]{3,2,1,0:T(8,128)(2,1)S(1)}, u32[]{:S(2)}, u32[]{:S(2)}) collective-permute-start(bf16[2,1,128,128]{3,2,1,0:T(8,128)(2,1)S(1)} %get-tuple-element.30), channel_id=1, source_target_pairs={{4,0},{8,4},{12,8},{5,1},{9,5},{13,9},{6,2},{10,6},{14,10},{7,3},{... | collective-permute-start | bytes 196616 | tf_op jit(solution)/shard_map/ppermute | solution.py:27
  172.0 19.8 %copy-start.5 = (f32[1,1,256,128]{3,2,1,0:T(8,128)S(1)}, f32[1,1,256,128]{3,2,1,0:T(8,128)}, u32[]{:S(2)}) copy-start(f32[1,1,256,128]{3,2,1,0:T(8,128)} %param.22) | copy-start | bytes 393220
Sparse Core Ops, SparseCore 0:
  29.3 19.4 all-reduce.10
  82.1 19.6 reduce-scatter.2
  119.2 16.0 all-reduce.12
  172.1 19.6 reduce-scatter.4
where the time goes:
time: 201 us; the launch traced here: 200 us
  waiting for transfers between devices  105 us (52%)
  blocking collectives  29.5 us (15%)
  starting transfers between devices  25.1 us (12%)
  between operations  15 us (7%)
  local copies, waits for them, and re-layouts  11.1 us (6%)
  other arithmetic  9.84 us (5%)
  matrix products  4.01 us (2%)
    reduce_scatter x2, waiting for transfers between devices, observe(): lax.psum_scatter(partial_term(cells).astype(jnp.bfloat16), 'space', scatt...  39.5 us
    psum x2, waiting for transfers between devices, adjoint(): total = lax.psum(local.astype(jnp.bfloat16), 'obs').astype(jnp.float32)  33.7 us
    all_gather x2, blocking collectives, spread_owned(): lax.all_gather(values.astype(jnp.bfloat16), 'space', axis=0, tiled=True)  29.5 us
    ppermute x4, waiting for transfers between devices, padded_2(): lax.ppermute(lax.slice_in_dim(block, 0, width, axis=dim), axis, backward)  17.1 us
    ppermute x4, starting transfers between devices, padded_2(): lax.ppermute(lax.slice_in_dim(block, block.shape[dim] - width, None, axis...  14.1 us
    ppermute x4, waiting for transfers between devices, from_behind(): return lax.ppermute(block, axis, route)  12.8 us
    ppermute x4, starting transfers between devices, from_behind(): return lax.ppermute(block, axis, route)  5.73 us
    ppermute x4, starting transfers between devices, padded_2(): lax.ppermute(lax.slice_in_dim(block, 0, width, axis=dim), axis, backward)  5.17 us
  transfers between devices with their start and end apart: 16, of which 16 were waited for; matrix products, arithmetic and copies ran while one was open for 1% of the time, Pallas kernels for 0%

commit v1 on v0

v1 whole, which is shorter than its diff:
```python
import functools

import jax
import jax.numpy as jnp
from jax import lax
from jax.experimental import pallas as pl
from jax.experimental.pallas import tpu as pltpu
from jax.sharding import PartitionSpec as P

MESH = pl.DeviceIdType.MESH

TW = 2
RD = 2

OCEAN = 0.35
SPATIAL = 0.2
TEMPORAL = 0.6
BF = jnp.bfloat16
F32 = jnp.float32


def kernel(
    n, nt, fp, which, order, land, sigma, dep, rinv, alpha, beta, inc, wout,
    fpt, spread, weights, cells, zsend, zrecv, psend, precv, osend, orecv, hsend, hrows, htime,
    zs, zr, ps, pr, os_, or_, hs, hr,
):
    s = lax.axis_index("space")
    k = lax.axis_index("tm")
    c = lax.axis_index("obs")
    cols = sigma.shape[1]
    low, high = s > 0, s < n - 1
    prev, nxt = k > 0, k < nt - 1
    both = jnp.logical_and

    hrows[...] = jnp.zeros_like(hrows)
    htime[...] = jnp.zeros_like(htime)

    barrier = pltpu.get_barrier_semaphore()
    partners = [(None, {"space": lax.rem(s + d, n)}) for d in range(1, n)]
    partners.append((None, {"obs": 1 - c}))
    partners.append((prev, {"tm": k - 1}))
    partners.append((nxt, {"tm": k + 1}))
    for sc, ds in ((low, -1), (high, 1)):
        for kc, dk in ((prev, -1), (nxt, 1)):
            partners.append((both(sc, kc), {"space": s + ds, "tm": k + dk}))

    def run_if(cond, action):
        if cond is None:
            action()
        else:
            pl.when(cond)(action)

    expected = 0
    for cond, target in partners:
        run_if(cond, functools.partial(
            pl.semaphore_signal, barrier, inc=1, device_id=target, device_id_type=MESH))
        expected = expected + (1 if cond is None else cond.astype(jnp.int32))

    scale = jnp.where(land[0] == 1, 1.0, OCEAN).astype(F32)
    for r in range(RD):
        spread[r] = jnp.broadcast_to(sigma[r:r + 1, :], (cols, cols)).T * scale
    height = weights.shape[0]
    lanes = weights.shape[1]
    for i in range(0, height, lanes):
        weights[i:i + lanes] = jnp.broadcast_to(rinv[0, :, i:i + lanes], (lanes, lanes)).T
    zsend[0] = (weights[...] * dep[0, 0]).astype(BF)

    pl.semaphore_wait(barrier, expected)
    pending = []

    def send(src, dst, ssem, rsem, target, cond=None):
        copy = pltpu.make_async_remote_copy(
            src_ref=src, dst_ref=dst, send_sem=ssem, recv_sem=rsem,
            device_id=target, device_id_type=MESH)
        run_if(cond, copy.start)
        pending.append((cond, copy))
        return copy

    def hops():
        return sorted(range(1, n), key=lambda d: -min(d, n - d))

    def gather_start(i):
        return {d: send(zsend.at[i], zrecv.at[i, d], zs.at[i, d], zr.at[i, d],
                        {"space": lax.rem(s + d, n)}) for d in hops()}

    def contribution(z, position):
        block = order[0, position]
        tile = which[0, 0, block]
        wide = z.astype(F32)
        parts = [wide * jnp.where(tile == t, 1.0, 0.0).astype(F32) for t in range(TW)]
        return jnp.dot(fpt[block], jnp.concatenate(parts, axis=1).astype(BF),
                       preferred_element_type=F32)

    def adjoint(i, copies):
        total = contribution(zsend[i], s)
        for d in reversed(hops()):
            copies[d].wait_recv()
            total = total + contribution(zrecv[i, d], lax.rem(s + n - d, n))
        for t in range(TW):
            osend[i, t] = total[:, t * lanes:(t + 1) * lanes].astype(BF)
        copy = send(osend.at[i], orecv.at[i], os_.at[i], or_.at[i], {"obs": 1 - c})
        copy.wait_recv()
        out = []
        for t in range(TW):
            tile = osend[i, t].astype(F32) + orecv[i, t].astype(F32)
            out.append([tile[r * cols:(r + 1) * cols] * spread[r] for r in range(RD)])
        return smooth(2 * i, out, False)

    def smooth(h, q, forward):
        for t in range(TW):
            for r in range(RD):
                hsend[h, t, r] = q[t][r].astype(BF)
        edge = TW - 1 if forward else 0
        step = 1 if forward else -1
        there, here = (nxt, prev) if forward else (prev, nxt)
        sides = ((high, low, 1, RD - 1, 0), (low, high, -1, 0, 1))
        waits = []
        for j, (to, frm, ds, row, side) in enumerate(sides):
            waits.append((frm, send(
                hsend.at[h, :, row], hrows.at[h, side, pl.ds(0, TW)], hs.at[h, j], hr.at[h, j],
                {"space": s + ds}, to)))
        for j, (to, frm, ds, row, side) in enumerate(sides):
            waits.append((both(frm, here), send(
                hsend.at[h, edge, row], hrows.at[h, side, TW], hs.at[h, 2 + j], hr.at[h, 2 + j],
                {"space": s + ds, "tm": k + step}, both(to, there))))
        waits.append((here, send(
            hsend.at[h, edge], htime.at[h], hs.at[h, 4], hr.at[h, 4], {"tm": k + step}, there)))
        for cond, copy in waits:
            run_if(cond, copy.wait_recv)
        at = lax.broadcasted_iota(jnp.int32, (cols, lanes), 0)
        out = []
        for t in range(TW):
            other = t - 1 if forward else t + 1
            inside = 0 <= other < TW
            slot = other if inside else TW
            rows = [hrows[h, 0, t].astype(F32) + TEMPORAL * hrows[h, 0, slot].astype(F32)]
            for r in range(RD):
                beside = q[other][r] if inside else htime[h, r].astype(F32)
                rows.append(q[t][r] + TEMPORAL * beside)
            rows.append(hrows[h, 1, t].astype(F32) + TEMPORAL * hrows[h, 1, slot].astype(F32))
            done = []
            for r in range(RD):
                u = rows[r + 1]
                left = jnp.where(at == 0, 0.0, pltpu.roll(u, 1, 0))
                right = jnp.where(at == cols - 1, 0.0, pltpu.roll(u, cols - 1, 0))
                done.append(u + SPATIAL * (rows[r] + rows[r + 2] + left + right))
            out.append(done)
        return out

    def correlate(h, field):
        done = smooth(h, field, True)
        return [[done[t][r] * spread[r] for r in range(RD)] for t in range(TW)]

    def observe(i, field):
        for t in range(TW):
            for r in range(RD):
                cells[i, t, r * cols:(r + 1) * cols] = field[t][r].astype(BF)

        def term(position):
            block = order[0, position]
            return jnp.dot(fp[0, 0, block], cells[i, which[0, 0, block]],
                           preferred_element_type=F32).astype(BF)

        copies = {}
        for d in hops():
            position = lax.rem(s + d, n)
            psend[i, d] = term(position)
            copies[d] = send(psend.at[i, d], precv.at[i, d], ps.at[i, d], pr.at[i, d],
                             {"space": position})
        total = term(s).astype(F32)
        for d in reversed(hops()):
            copies[d].wait_recv()
            total = total + precv[i, d].astype(F32)
        return total

    copies = gather_start(0)
    for b in range(n):
        fpt[b] = fp[0, 0, b].T
    gradient = adjoint(0, copies)
    zsend[1] = (weights[...] * observe(0, correlate(1, gradient))).astype(BF)
    image = adjoint(1, gather_start(1))
    first, second, turn = alpha[0:1, :], alpha[1:2, :], beta[0:1, :]
    state = []
    for t in range(TW):
        rows = []
        for r in range(RD):
            g = gradient[t][r]
            residual = g - first * (g + image[t][r])
            rows.append(first * g + second * (residual + turn * g))
        state.append(rows)
    increment = correlate(3, state)
    for t in range(TW):
        for r in range(RD):
            inc[t, r] = increment[t][r]
    fitted = observe(1, increment)
    wout[0, 0] = weights[...] * (fitted - dep[0, 0])
    for cond, copy in pending:
        run_if(cond, copy.wait_send)


def solution(mesh):
    n, nt = mesh.shape["space"], mesh.shape["tm"]

    def shards(footprint, tile_index, assign, land, sigma, departures, rinv, alpha, beta):
        blocks, width = footprint.shape[2], footprint.shape[3]
        cols, members = sigma.shape[1], alpha.shape[1]
        assert blocks == n and width == RD * cols and sigma.shape[0] == RD
        vmem = pl.BlockSpec(memory_space=pltpu.VMEM)
        smem = pl.BlockSpec(memory_space=pltpu.SMEM)
        dma = pltpu.SemaphoreType.DMA
        return pl.pallas_call(
            functools.partial(kernel, n, nt),
            out_shape=(
                jax.ShapeDtypeStruct((TW, RD, cols, members), F32),
                jax.ShapeDtypeStruct((1, 1, width, members), F32),
            ),
            in_specs=[vmem, smem, smem, smem, vmem, vmem, vmem, vmem, vmem],
            out_specs=(vmem, vmem),
            scratch_shapes=[
                pltpu.VMEM((n, width, width), BF),
                pltpu.VMEM((RD, cols, members), F32),
                pltpu.VMEM((width, members), F32),
                pltpu.VMEM((2, TW, width, members), BF),
                pltpu.VMEM((2, width, members), BF),
                pltpu.VMEM((2, n, width, members), BF),
                pltpu.VMEM((2, n, width, members), BF),
                pltpu.VMEM((2, n, width, members), BF),
                pltpu.VMEM((2, TW, width, members), BF),
                pltpu.VMEM((2, TW, width, members), BF),
                pltpu.VMEM((4, TW, RD, cols, members), BF),
                pltpu.VMEM((4, 2, TW + 1, cols, members), BF),
                pltpu.VMEM((4, RD, cols, members), BF),
                dma((2, n)), dma((2, n)), dma((2, n)), dma((2, n)),
                dma((2,)), dma((2,)), dma((4, 5)), dma((4, 5)),
            ],
            compiler_params=pltpu.CompilerParams(
                collective_id=0, has_side_effects=True, vmem_limit_bytes=40 * 1024 * 1024
            ),
        )(footprint, tile_index, assign, land, sigma, departures, rinv, alpha, beta)

    in_specs = (
        P("space", ("tm", "obs"), None, None, None),
        P(("groups", "space"), ("tm", "obs"), None),
        P(("groups", "tm", "obs"), None),
        P("space"),
        P(("groups", "space"), None),
        P(("groups", "tm", "obs"), "space", None, None),
        P(("groups", "tm", "obs"), "space", None),
        P("groups", None),
        P("groups", None),
    )
    out_specs = (
        P(("groups", "tm"), "space", None, None),
        P(("groups", "tm", "obs"), "space", None, None),
    )
    return jax.shard_map(shards, mesh=mesh, in_specs=in_specs, out_specs=out_specs, check_vma=False)
```

time: 201 us -> 61.4 us (0.31)
  waiting for transfers between devices: 105 us -> 0 us
  Pallas kernels: 0 us -> 53.8 us
  blocking collectives: 29.5 us -> 0 us
  starting transfers between devices: 25.1 us -> 0 us
  between operations: 15 us -> 1.35 us
  other arithmetic: 9.84 us -> 0 us
  local copies, waits for them, and re-layouts: 11.1 us -> 5.97 us
  matrix products: 4.01 us -> 0 us
    pallas_call x0 -> x1, Pallas kernels: none -> 53.8 us  [shards(): pl.pallas_call(functools.partial(kernel, n, nt), out_shape=(jax.ShapeDtyp...]
    reduce_scatter x2 -> x0, waiting for transfers between devices: 39.5 us -> none  [observe(): lax.psum_scatter(partial_term(cells).astype(jnp.bfloat16), 'space', scatt...]
    psum x2 -> x0, waiting for transfers between devices: 33.7 us -> none  [adjoint(): total = lax.psum(local.astype(jnp.bfloat16), 'obs').astype(jnp.float32)]
    ppermute x12 -> x0, waiting for transfers between devices: 32 us -> none  [the longest x4 17.1 us: padded_2(): lax.ppermute(lax.slice_in_dim(block, 0, width, axis=dim), axis, backward)]
    all_gather x2 -> x0, blocking collectives: 29.5 us -> none  [spread_owned(): lax.all_gather(values.astype(jnp.bfloat16), 'space', axis=0, tiled=True)]
    ppermute x12 -> x0, starting transfers between devices: 25 us -> none  [the longest x4 14.1 us: padded_2(): lax.ppermute(lax.slice_in_dim(block, block.shape[dim] - width, None, axis...]
    convert_element_type x14 -> x0, other arithmetic: 4.14 us -> none  [the longest x2 1.93 us: spread_owned(): values.astype(jnp.bfloat16)]
    dot_general x6 -> x0, matrix products: 4.01 us -> none  [the longest x2 2.13 us: partial_term(): jnp.einsum('bij,bjm->bim', picked, inputs, preferred_element_type=jnp.flo...]
  transfers between devices with their start and end apart: 16 -> 0, of which waited for: 16 -> 0; matrix products, arithmetic and copies ran while one was open for 1% -> 0% of each run, Pallas kernels for 0% -> 0%
where the time goes in v1:
time: 61.4 us; the launch traced here: 61.1 us
  Pallas kernels  53.8 us (88%)
  local copies, waits for them, and re-layouts  5.97 us (10%)
  between operations  1.35 us (2%)
    pallas_call x1, Pallas kernels, shards(): pl.pallas_call(functools.partial(kernel, n, nt), out_shape=(jax.ShapeDtyp...  53.8 us
    unnamed x18, local copies, waits for them, and re-layouts  5.97 us

profile of v1, /device:TPU:0, one launch (start us, length us, event | category | flops | bytes accessed | tf_op | source)
XLA Modules:
  0.0 61.1 jit_solution(6710830790209642674)
XLA Ops:
  0.6 0.0 copy-start.2
  0.6 0.0 copy-start.5
  1.3 0.0 copy-done.2
  1.3 0.0 copy-done.5
  1.3 0.0 copy-start
  1.3 1.0 %copy-done = bf16[1,1,4,256,256]{4,3,2,1,0:T(8,128)(2,1)S(1)} copy-done((bf16[1,1,4,256,256]{4,3,2,1,0:T(8,128)(2,1)S(1)}, bf16[1,1,4,256,256]{4,3,2,1,0:T(8,128)(2,1)}, u32[]{:S(2)}) %copy-start) | copy-done | bytes 524312
  2.4 0.0 copy-start.1
  2.4 0.9 %copy-done.1 = f32[1,1,256,128]{3,2,1,0:T(8,128)S(1)} copy-done((f32[1,1,256,128]{3,2,1,0:T(8,128)S(1)}, f32[1,1,256,128]{3,2,1,0:T(8,128)}, u32[]{:S(2)}) %copy-start.1) | copy-done | bytes 131096
  3.3 0.0 copy-start.3
  3.3 0.7 %copy-done.3 = f32[1,1,256]{2,1,0:T(1,128)S(1)} copy-done((f32[1,1,256]{2,1,0:T(1,128)S(1)}, f32[1,1,256]{2,1,0:T(1,128)}, u32[]{:S(2)}) %copy-start.3) | copy-done | bytes 1048
  4.0 0.0 copy-start.4
  4.0 0.7 %copy-done.4 = f32[2,128]{1,0:T(2,128)S(1)} copy-done((f32[2,128]{1,0:T(2,128)S(1)}, f32[2,128]{1,0:T(2,128)}, u32[]{:S(2)}) %copy-start.4) | copy-done | bytes 1048
  4.6 0.0 copy-start.6
  4.6 0.7 %copy-done.6 = s32[1,4]{1,0:T(1,128)S(1)} copy-done((s32[1,4]{1,0:T(1,128)S(1)}, s32[1,4]{1,0:T(1,128)}, u32[]{:S(2)}) %copy-start.6) | copy-done | bytes 40
  5.3 0.0 copy-start.7
  5.3 0.7 %copy-done.7 = f32[1,128]{1,0:T(1,128)S(1)} copy-done((f32[1,128]{1,0:T(1,128)S(1)}, f32[1,128]{1,0:T(1,128)}, u32[]{:S(2)}) %copy-start.7) | copy-done | bytes 536
  6.0 53.8 %shard_map.104 = (f32[2,2,128,128]{3,2,1,0:T(8,128)S(1)}, f32[1,1,256,128]{3,2,1,0:T(8,128)S(1)}) custom-call(bf16[1,1,4,256,256]{4,3,2,1,0:T(8,128)(2,1)S(1)} %copy-done, s32[1,1,4]{2,1,0:T(1,128)S(1)} %copy-done.5, s32[1,4]{1,0:T(1,128)S(1)} %copy-done.6, s32[1]{0:T(128)S(6)} %copy.13.land, f32[2,128]{1,0:T(2,128)S(1)} %copy-done.2, ...), custom_call_target="tpu_custom_call" | custom-call | tf_op jit(solution)/shard_map/pallas_call | solution.py:211
  59.8 0.7 %copy.14 = f32[2,2,128,128]{3,2,1,0:T(8,128)} copy(f32[2,2,128,128]{3,2,1,0:T(8,128)S(1)} %get-tuple-element.4) | data formatting | bytes 524288
  60.5 0.7 %copy.15 = f32[1,1,256,128]{3,2,1,0:T(8,128)} copy(f32[1,1,256,128]{3,2,1,0:T(8,128)S(1)} %get-tuple-element.5) | data formatting | bytes 262144
Async XLA Ops:
  0.6 0.7 %copy-start.2 = (f32[2,128]{1,0:T(2,128)S(1)}, f32[2,128]{1,0:T(2,128)}, u32[]{:S(2)}) copy-start(f32[2,128]{1,0:T(2,128)} %sigma.1) | copy-start | bytes 3076
  0.6 0.7 %copy-start.5 = (s32[1,1,4]{2,1,0:T(1,128)S(1)}, s32[1,1,4]{2,1,0:T(1,128)}, u32[]{:S(2)}) copy-start(s32[1,1,4]{2,1,0:T(1,128)} %which.1) | copy-start | bytes 52
  1.3 1.0 %copy-start = (bf16[1,1,4,256,256]{4,3,2,1,0:T(8,128)(2,1)S(1)}, bf16[1,1,4,256,256]{4,3,2,1,0:T(8,128)(2,1)}, u32[]{:S(2)}) copy-start(bf16[1,1,4,256,256]{4,3,2,1,0:T(8,128)(2,1)} %fp.1) | copy-start | bytes 1572868
  2.4 0.9 %copy-start.1 = (f32[1,1,256,128]{3,2,1,0:T(8,128)S(1)}, f32[1,1,256,128]{3,2,1,0:T(8,128)}, u32[]{:S(2)}) copy-start(f32[1,1,256,128]{3,2,1,0:T(8,128)} %dep.1) | copy-start | bytes 393220
  3.3 0.7 %copy-start.3 = (f32[1,1,256]{2,1,0:T(1,128)S(1)}, f32[1,1,256]{2,1,0:T(1,128)}, u32[]{:S(2)}) copy-start(f32[1,1,256]{2,1,0:T(1,128)} %rinv.1) | copy-start | bytes 3076
  4.0 0.7 %copy-start.4 = (f32[2,128]{1,0:T(2,128)S(1)}, f32[2,128]{1,0:T(2,128)}, u32[]{:S(2)}) copy-start(f32[2,128]{1,0:T(2,128)} %alpha.1) | copy-start | bytes 3076
  4.6 0.7 %copy-start.6 = (s32[1,4]{1,0:T(1,128)S(1)}, s32[1,4]{1,0:T(1,128)}, u32[]{:S(2)}) copy-start(s32[1,4]{1,0:T(1,128)} %order.1) | copy-start | bytes 52
  5.3 0.7 %copy-start.7 = (f32[1,128]{1,0:T(1,128)S(1)}, f32[1,128]{1,0:T(1,128)}, u32[]{:S(2)}) copy-start(f32[1,128]{1,0:T(1,128)} %beta.1) | copy-start | bytes 1540

commit v2 on v1

--- a/solution.py
+++ b/solution.py
@@ -20,8 +20,8 @@
 
 
 def kernel(
-    n, nt, fp, which, order, land, sigma, dep, rinv, alpha, beta, inc, wout,
-    fpt, spread, weights, cells, zsend, zrecv, psend, precv, osend, orecv, hsend, hrows, htime,
+    n, nt, fp_in, which_in, order_in, land_in, sigma_in, dep_in, rinv_in, alpha_in, beta_in,
+    inc, wout, fp, which, order, land, sigma, dep, rinv, alpha, beta, loaded, fpt, spread, weights, cells, zsend, zrecv, psend, precv, osend, orecv, hsend, hrows, htime,
     zs, zr, ps, pr, os_, or_, hs, hr,
 ):
     s = lax.axis_index("space")
@@ -32,6 +32,12 @@
     prev, nxt = k > 0, k < nt - 1
     both = jnp.logical_and
 
+    loads = [pltpu.make_async_copy(src, dst, loaded.at[j]) for j, (src, dst) in enumerate((
+        (sigma_in, sigma), (rinv_in, rinv), (dep_in, dep), (land_in, land), (order_in, order),
+        (which_in, which), (alpha_in, alpha), (beta_in, beta), (fp_in, fp)))]
+    for load in loads:
+        load.start()
+
     hrows[...] = jnp.zeros_like(hrows)
     htime[...] = jnp.zeros_like(htime)
 
@@ -56,6 +62,8 @@
             pl.semaphore_signal, barrier, inc=1, device_id=target, device_id_type=MESH))
         expected = expected + (1 if cond is None else cond.astype(jnp.int32))
 
+    for load in loads[:-1]:
+        load.wait()
     scale = jnp.where(land[0] == 1, 1.0, OCEAN).astype(F32)
     for r in range(RD):
         spread[r] = jnp.broadcast_to(sigma[r:r + 1, :], (cols, cols)).T * scale
@@ -174,6 +182,7 @@
         return total
 
     copies = gather_start(0)
+    loads[-1].wait()
     for b in range(n):
         fpt[b] = fp[0, 0, b].T
     gradient = adjoint(0, copies)
@@ -206,7 +215,9 @@
         cols, members = sigma.shape[1], alpha.shape[1]
         assert blocks == n and width == RD * cols and sigma.shape[0] == RD
         vmem = pl.BlockSpec(memory_space=pltpu.VMEM)
-        smem = pl.BlockSpec(memory_space=pltpu.SMEM)
+        outside = pl.BlockSpec(memory_space=pltpu.HBM)
+        operands = (footprint, tile_index, assign, land, sigma, departures, rinv, alpha, beta)
+        scalars = (tile_index, assign, land)
         dma = pltpu.SemaphoreType.DMA
         return pl.pallas_call(
             functools.partial(kernel, n, nt),
@@ -214,9 +225,12 @@
                 jax.ShapeDtypeStruct((TW, RD, cols, members), F32),
                 jax.ShapeDtypeStruct((1, 1, width, members), F32),
             ),
-            in_specs=[vmem, smem, smem, smem, vmem, vmem, vmem, vmem, vmem],
+            in_specs=[outside] * len(operands),
             out_specs=(vmem, vmem),
             scratch_shapes=[
+                *((pltpu.SMEM if any(a is b for b in scalars) else pltpu.VMEM)(a.shape, a.dtype)
+                  for a in operands),
+                dma((len(operands),)),
                 pltpu.VMEM((n, width, width), BF),
                 pltpu.VMEM((RD, cols, members), F32),
                 pltpu.VMEM((width, members), F32),
@@ -234,9 +248,9 @@
                 dma((2,)), dma((2,)), dma((4, 5)), dma((4, 5)),
             ],
             compiler_params=pltpu.CompilerParams(
-                collective_id=0, has_side_effects=True, vmem_limit_bytes=40 * 1024 * 1024
+                collective_id=0, has_side_effects=True, vmem_limit_bytes=63 * 1024 * 1024
             ),
-        )(footprint, tile_index, assign, land, sigma, departures, rinv, alpha, beta)
+        )(*operands)
 
     in_specs = (
         P("space", ("tm", "obs"), None, None, None),

time: 61.4 us -> 59 us (0.961)
  local copies, waits for them, and re-layouts: 5.97 us -> 2.36 us
  Pallas kernels: 53.8 us -> 55.2 us
    unnamed x18 -> x4, local copies, waits for them, and re-layouts: 5.97 us -> 2.36 us
    pallas_call x1, Pallas kernels: 53.8 us -> 55.2 us  [shards(): pl.pallas_call(functools.partial(kernel, n, nt), out_shape=(jax.ShapeDtyp...]
where the time goes in v2:
time: 59 us; the launch traced here: 58.8 us
  Pallas kernels  55.2 us (94%)
  local copies, waits for them, and re-layouts  2.36 us (4%)
  between operations  1.29 us (2%)
    pallas_call x1, Pallas kernels, shards(): pl.pallas_call(functools.partial(kernel, n, nt), out_shape=(jax.ShapeDtyp...  55.2 us
    unnamed x4, local copies, waits for them, and re-layouts  2.36 us

profile of v2, /device:TPU:0, one launch (start us, length us, event | category | flops | bytes accessed | tf_op | source)
XLA Modules:
  0.0 58.8 jit_solution(13780518439689778063)
XLA Ops:
  1.3 55.2 %shard_map.104 = (f32[2,2,128,128]{3,2,1,0:T(8,128)}, f32[1,1,256,128]{3,2,1,0:T(8,128)}) custom-call(bf16[1,1,4,256,256]{4,3,2,1,0:T(8,128)(2,1)} %fp_in.1, s32[1,1,4]{2,1,0:T(1,128)} %which_in.1, s32[1,4]{1,0:T(1,128)} %order_in.1, s32[1]{0:T(128)S(6)} %copy.13.land_in, f32[2,128]{1,0:T(2,128)} %sigma_in.1, f32[1,1,256,128]{3,2,1,0:T(8,128)} %dep_in.1, ...), custom_call_target="tpu_custom_call" | custom-call | tf_op jit(solution)/shard_map/pallas_call | solution.py:222
  56.4 0.0 copy-start
  56.4 1.7 %copy.14 = f32[2,2,128,128]{3,2,1,0:T(8,128)} copy(f32[2,2,128,128]{3,2,1,0:T(8,128)} %get-tuple-element.4) | data formatting | bytes 524288
  58.2 0.0 copy-done
  58.2 0.7 %copy.15 = f32[1,1,256,128]{3,2,1,0:T(8,128)} copy(f32[1,1,256,128]{3,2,1,0:T(8,128)S(1)} %copy-done) | data formatting | bytes 262144
Async XLA Ops:
  56.4 1.7 %copy-start = (f32[1,1,256,128]{3,2,1,0:T(8,128)S(1)}, f32[1,1,256,128]{3,2,1,0:T(8,128)}, u32[]{:S(2)}) copy-start(f32[1,1,256,128]{3,2,1,0:T(8,128)} %get-tuple-element.5) | copy-start | bytes 393220

commit v3 on v2

--- a/solution.py
+++ b/solution.py
@@ -21,7 +21,7 @@
 
 def kernel(
     n, nt, fp_in, which_in, order_in, land_in, sigma_in, dep_in, rinv_in, alpha_in, beta_in,
-    inc, wout, fp, which, order, land, sigma, dep, rinv, alpha, beta, loaded, fpt, spread, weights, cells, zsend, zrecv, psend, precv, osend, orecv, hsend, hrows, htime,
+    inc, wout, fp, which, order, land, sigma, dep, rinv, alpha, beta, loaded, fpt, spread, weights, cells, zsend, zrecv, psend, precv, osend, orecv, hsend, hrows, htime, part,
     zs, zr, ps, pr, os_, or_, hs, hr,
 ):
     s = lax.axis_index("space")
@@ -31,6 +31,7 @@
     low, high = s > 0, s < n - 1
     prev, nxt = k > 0, k < nt - 1
     both = jnp.logical_and
+    relay = n == 4
 
     loads = [pltpu.make_async_copy(src, dst, loaded.at[j]) for j, (src, dst) in enumerate((
         (sigma_in, sigma), (rinv_in, rinv), (dep_in, dep), (land_in, land), (order_in, order),
@@ -88,8 +89,23 @@
         return sorted(range(1, n), key=lambda d: -min(d, n - d))
 
     def gather_start(i):
-        return {d: send(zsend.at[i], zrecv.at[i, d], zs.at[i, d], zr.at[i, d],
-                        {"space": lax.rem(s + d, n)}) for d in hops()}
+        copies = {}
+        for d in hops():
+            copies[d] = (ends_only if relay and d == 2 else send)(
+                zsend.at[i], zrecv.at[i, d], zs.at[i, d], zr.at[i, d],
+                {"space": lax.rem(s + d, n)})
+        return copies
+
+    def ends_only(src, dst, ssem, rsem, target):
+        at_end = jnp.logical_or(s == 0, s == n - 1)
+        return send(src, dst, ssem, rsem, target, at_end)
+
+    def pass_on(i, d):
+        if not relay or d == 2:
+            return
+        target = 3 if d == 1 else 0
+        send(zrecv.at[i, d], zrecv.at[i, 2], zs.at[i, 2], zr.at[i, 2], {"space": target},
+             s == (2 if d == 1 else 1))
 
     def contribution(z, position):
         block = order[0, position]
@@ -101,8 +117,13 @@
 
     def adjoint(i, copies):
         total = contribution(zsend[i], s)
+        early = [d for d in reversed(hops()) if relay and d != 2]
+        for d in early:
+            copies[d].wait_recv()
+            pass_on(i, d)
         for d in reversed(hops()):
-            copies[d].wait_recv()
+            if d not in early:
+                copies[d].wait_recv()
             total = total + contribution(zrecv[i, d], lax.rem(s + n - d, n))
         for t in range(TW):
             osend[i, t] = total[:, t * lanes:(t + 1) * lanes].astype(BF)
@@ -124,34 +145,49 @@
         sides = ((high, low, 1, RD - 1, 0), (low, high, -1, 0, 1))
         waits = []
         for j, (to, frm, ds, row, side) in enumerate(sides):
+            waits.append((both(frm, here), send(
+                hsend.at[h, edge, row], hrows.at[h, side, TW], hs.at[h, 2 + j], hr.at[h, 2 + j],
+                {"space": s + ds, "tm": k + step}, both(to, there))))
+        last = (here, send(
+            hsend.at[h, edge], htime.at[h], hs.at[h, 4], hr.at[h, 4], {"tm": k + step}, there))
+        for j, (to, frm, ds, row, side) in enumerate(sides):
             waits.append((frm, send(
                 hsend.at[h, :, row], hrows.at[h, side, pl.ds(0, TW)], hs.at[h, j], hr.at[h, j],
                 {"space": s + ds}, to)))
-        for j, (to, frm, ds, row, side) in enumerate(sides):
-            waits.append((both(frm, here), send(
-                hsend.at[h, edge, row], hrows.at[h, side, TW], hs.at[h, 2 + j], hr.at[h, 2 + j],
-                {"space": s + ds, "tm": k + step}, both(to, there))))
-        waits.append((here, send(
-            hsend.at[h, edge], htime.at[h], hs.at[h, 4], hr.at[h, 4], {"tm": k + step}, there)))
+        at = lax.broadcasted_iota(jnp.int32, (cols, lanes), 0)
+        other = [t - 1 if forward else t + 1 for t in range(TW)]
+        inside = [0 <= o < TW for o in other]
+
+        def own(t):
+            us = []
+            for r in range(RD):
+                beside = q[other[t]][r] if inside[t] else htime[h, r].astype(F32)
+                us.append(q[t][r] + TEMPORAL * beside)
+            for r in range(RD):
+                u = us[r]
+                total = jnp.where(at == 0, 0.0, pltpu.roll(u, 1, 0))
+                total = total + jnp.where(at == cols - 1, 0.0, pltpu.roll(u, cols - 1, 0))
+                for near in (r - 1, r + 1):
+                    if 0 <= near < RD:
+                        total = total + us[near]
+                part[t, r] = u + SPATIAL * total
+
+        for t in range(TW):
+            if inside[t]:
+                own(t)
+        run_if(last[0], last[1].wait_recv)
+        for t in range(TW):
+            if not inside[t]:
+                own(t)
         for cond, copy in waits:
             run_if(cond, copy.wait_recv)
-        at = lax.broadcasted_iota(jnp.int32, (cols, lanes), 0)
         out = []
         for t in range(TW):
-            other = t - 1 if forward else t + 1
-            inside = 0 <= other < TW
-            slot = other if inside else TW
-            rows = [hrows[h, 0, t].astype(F32) + TEMPORAL * hrows[h, 0, slot].astype(F32)]
-            for r in range(RD):
-                beside = q[other][r] if inside else htime[h, r].astype(F32)
-                rows.append(q[t][r] + TEMPORAL * beside)
-            rows.append(hrows[h, 1, t].astype(F32) + TEMPORAL * hrows[h, 1, slot].astype(F32))
-            done = []
-            for r in range(RD):
-                u = rows[r + 1]
-                left = jnp.where(at == 0, 0.0, pltpu.roll(u, 1, 0))
-                right = jnp.where(at == cols - 1, 0.0, pltpu.roll(u, cols - 1, 0))
-                done.append(u + SPATIAL * (rows[r] + rows[r + 2] + left + right))
+            slot = other[t] if inside[t] else TW
+            done = [part[t, r] for r in range(RD)]
+            for side, r in ((0, 0), (1, RD - 1)):
+                beyond = hrows[h, side, t].astype(F32) + TEMPORAL * hrows[h, side, slot].astype(F32)
+                done[r] = done[r] + SPATIAL * beyond
             out.append(done)
         return out
 
@@ -244,6 +280,7 @@
                 pltpu.VMEM((4, TW, RD, cols, members), BF),
                 pltpu.VMEM((4, 2, TW + 1, cols, members), BF),
                 pltpu.VMEM((4, RD, cols, members), BF),
+                pltpu.VMEM((TW, RD, cols, members), F32),
                 dma((2, n)), dma((2, n)), dma((2, n)), dma((2, n)),
                 dma((2,)), dma((2,)), dma((4, 5)), dma((4, 5)),
             ],

time: 59 us -> 59.6 us (1.010)
  Pallas kernels: 55.2 us -> 55.8 us
    pallas_call x1, Pallas kernels: 55.2 us -> 55.8 us  [shards(): pl.pallas_call(functools.partial(kernel, n, nt), out_shape=(jax.ShapeDtyp...]
where the time goes in v3:
time: 59.6 us; the launch traced here: 59.4 us
  Pallas kernels  55.8 us (94%)
  local copies, waits for them, and re-layouts  2.36 us (4%)
  between operations  1.29 us (2%)
    pallas_call x1, Pallas kernels, shards(): pl.pallas_call(functools.partial(kernel, n, nt), out_shape=(jax.ShapeDtyp...  55.8 us
    unnamed x4, local copies, waits for them, and re-layouts  2.36 us

profile of v3, /device:TPU:0, one launch (start us, length us, event | category | flops | bytes accessed | tf_op | source)
XLA Modules:
  0.0 59.4 jit_solution(14178690474744641403)
XLA Ops:
  1.3 55.8 %shard_map.104 = (f32[2,2,128,128]{3,2,1,0:T(8,128)}, f32[1,1,256,128]{3,2,1,0:T(8,128)}) custom-call(bf16[1,1,4,256,256]{4,3,2,1,0:T(8,128)(2,1)} %fp_in.1, s32[1,1,4]{2,1,0:T(1,128)} %which_in.1, s32[1,4]{1,0:T(1,128)} %order_in.1, s32[1]{0:T(128)S(6)} %copy.13.land_in, f32[2,128]{1,0:T(2,128)} %sigma_in.1, f32[1,1,256,128]{3,2,1,0:T(8,128)} %dep_in.1, ...), custom_call_target="tpu_custom_call" | custom-call | tf_op jit(solution)/shard_map/pallas_call | solution.py:258
  57.1 0.0 copy-start
  57.1 1.7 %copy.14 = f32[2,2,128,128]{3,2,1,0:T(8,128)} copy(f32[2,2,128,128]{3,2,1,0:T(8,128)} %get-tuple-element.4) | data formatting | bytes 524288
  58.8 0.0 copy-done
  58.8 0.7 %copy.15 = f32[1,1,256,128]{3,2,1,0:T(8,128)} copy(f32[1,1,256,128]{3,2,1,0:T(8,128)S(1)} %copy-done) | data formatting | bytes 262144
Async XLA Ops:
  57.1 1.7 %copy-start = (f32[1,1,256,128]{3,2,1,0:T(8,128)S(1)}, f32[1,1,256,128]{3,2,1,0:T(8,128)}, u32[]{:S(2)}) copy-start(f32[1,1,256,128]{3,2,1,0:T(8,128)} %get-tuple-element.5) | copy-start | bytes 393220

commit v4 on v3

--- a/solution.py
+++ b/solution.py
@@ -21,7 +21,7 @@
 
 def kernel(
     n, nt, fp_in, which_in, order_in, land_in, sigma_in, dep_in, rinv_in, alpha_in, beta_in,
-    inc, wout, fp, which, order, land, sigma, dep, rinv, alpha, beta, loaded, fpt, spread, weights, cells, zsend, zrecv, psend, precv, osend, orecv, hsend, hrows, htime, part,
+    inc_out, w_out, inc, wout, stored, fp, which, order, land, sigma, dep, rinv, alpha, beta, loaded, fpt, spread, weights, cells, zsend, zrecv, psend, precv, osend, orecv, hsend, hrows, htime, part,
     zs, zr, ps, pr, os_, or_, hs, hr,
 ):
     s = lax.axis_index("space")
@@ -31,7 +31,6 @@
     low, high = s > 0, s < n - 1
     prev, nxt = k > 0, k < nt - 1
     both = jnp.logical_and
-    relay = n == 4
 
     loads = [pltpu.make_async_copy(src, dst, loaded.at[j]) for j, (src, dst) in enumerate((
         (sigma_in, sigma), (rinv_in, rinv), (dep_in, dep), (land_in, land), (order_in, order),
@@ -89,23 +88,8 @@
         return sorted(range(1, n), key=lambda d: -min(d, n - d))
 
     def gather_start(i):
-        copies = {}
-        for d in hops():
-            copies[d] = (ends_only if relay and d == 2 else send)(
-                zsend.at[i], zrecv.at[i, d], zs.at[i, d], zr.at[i, d],
-                {"space": lax.rem(s + d, n)})
-        return copies
-
-    def ends_only(src, dst, ssem, rsem, target):
-        at_end = jnp.logical_or(s == 0, s == n - 1)
-        return send(src, dst, ssem, rsem, target, at_end)
-
-    def pass_on(i, d):
-        if not relay or d == 2:
-            return
-        target = 3 if d == 1 else 0
-        send(zrecv.at[i, d], zrecv.at[i, 2], zs.at[i, 2], zr.at[i, 2], {"space": target},
-             s == (2 if d == 1 else 1))
+        return {d: send(zsend.at[i], zrecv.at[i, d], zs.at[i, d], zr.at[i, d],
+                        {"space": lax.rem(s + d, n)}) for d in hops()}
 
     def contribution(z, position):
         block = order[0, position]
@@ -117,13 +101,8 @@
 
     def adjoint(i, copies):
         total = contribution(zsend[i], s)
-        early = [d for d in reversed(hops()) if relay and d != 2]
-        for d in early:
+        for d in reversed(hops()):
             copies[d].wait_recv()
-            pass_on(i, d)
-        for d in reversed(hops()):
-            if d not in early:
-                copies[d].wait_recv()
             total = total + contribution(zrecv[i, d], lax.rem(s + n - d, n))
         for t in range(TW):
             osend[i, t] = total[:, t * lanes:(t + 1) * lanes].astype(BF)
@@ -237,8 +216,14 @@
     for t in range(TW):
         for r in range(RD):
             inc[t, r] = increment[t][r]
+    inc_copy = pltpu.make_async_copy(inc, inc_out, stored.at[0])
+    inc_copy.start()
     fitted = observe(1, increment)
     wout[0, 0] = weights[...] * (fitted - dep[0, 0])
+    w_copy = pltpu.make_async_copy(wout, w_out, stored.at[1])
+    w_copy.start()
+    inc_copy.wait()
+    w_copy.wait()
     for cond, copy in pending:
         run_if(cond, copy.wait_send)
 
@@ -250,7 +235,6 @@
         blocks, width = footprint.shape[2], footprint.shape[3]
         cols, members = sigma.shape[1], alpha.shape[1]
         assert blocks == n and width == RD * cols and sigma.shape[0] == RD
-        vmem = pl.BlockSpec(memory_space=pltpu.VMEM)
         outside = pl.BlockSpec(memory_space=pltpu.HBM)
         operands = (footprint, tile_index, assign, land, sigma, departures, rinv, alpha, beta)
         scalars = (tile_index, assign, land)
@@ -262,8 +246,11 @@
                 jax.ShapeDtypeStruct((1, 1, width, members), F32),
             ),
             in_specs=[outside] * len(operands),
-            out_specs=(vmem, vmem),
+            out_specs=(outside, outside),
             scratch_shapes=[
+                pltpu.VMEM((TW, RD, cols, members), F32),
+                pltpu.VMEM((1, 1, width, members), F32),
+                dma((2,)),
                 *((pltpu.SMEM if any(a is b for b in scalars) else pltpu.VMEM)(a.shape, a.dtype)
                   for a in operands),
                 dma((len(operands),)),

time: 59.6 us -> 57.9 us (0.971)
  Pallas kernels: 55.8 us -> 54.1 us
    pallas_call x1, Pallas kernels: 55.8 us -> 54.1 us  [shards(): pl.pallas_call(functools.partial(kernel, n, nt), out_shape=(jax.ShapeDtyp...]
where the time goes in v4:
time: 57.9 us; the launch traced here: 57.7 us
  Pallas kernels  54.1 us (93%)
  local copies, waits for them, and re-layouts  2.36 us (4%)
  between operations  1.29 us (2%)
    pallas_call x1, Pallas kernels, shards(): pl.pallas_call(functools.partial(kernel, n, nt), out_shape=(jax.ShapeDtyp...  54.1 us
    unnamed x4, local copies, waits for them, and re-layouts  2.36 us

profile of v4, /device:TPU:0, one launch (start us, length us, event | category | flops | bytes accessed | tf_op | source)
XLA Modules:
  0.0 57.7 jit_solution(9752264245331339758)
XLA Ops:
  1.3 54.1 %shard_map.104 = (f32[2,2,128,128]{3,2,1,0:T(8,128)}, f32[1,1,256,128]{3,2,1,0:T(8,128)}) custom-call(bf16[1,1,4,256,256]{4,3,2,1,0:T(8,128)(2,1)} %fp_in.1, s32[1,1,4]{2,1,0:T(1,128)} %which_in.1, s32[1,4]{1,0:T(1,128)} %order_in.1, s32[1]{0:T(128)S(6)} %copy.13.land_in, f32[2,128]{1,0:T(2,128)} %sigma_in.1, f32[1,1,256,128]{3,2,1,0:T(8,128)} %dep_in.1, ...), custom_call_target="tpu_custom_call" | custom-call | tf_op jit(solution)/shard_map/pallas_call | solution.py:242
  55.3 0.0 copy-start
  55.4 1.7 %copy.14 = f32[2,2,128,128]{3,2,1,0:T(8,128)} copy(f32[2,2,128,128]{3,2,1,0:T(8,128)} %get-tuple-element.4) | data formatting | bytes 524288
  57.1 0.0 copy-done
  57.1 0.7 %copy.15 = f32[1,1,256,128]{3,2,1,0:T(8,128)} copy(f32[1,1,256,128]{3,2,1,0:T(8,128)S(1)} %copy-done) | data formatting | bytes 262144
Async XLA Ops:
  55.3 1.7 %copy-start = (f32[1,1,256,128]{3,2,1,0:T(8,128)S(1)}, f32[1,1,256,128]{3,2,1,0:T(8,128)}, u32[]{:S(2)}) copy-start(f32[1,1,256,128]{3,2,1,0:T(8,128)} %get-tuple-element.5) | copy-start | bytes 393220

commit v5 on v4

--- a/solution.py
+++ b/solution.py
@@ -104,31 +104,42 @@
         for d in reversed(hops()):
             copies[d].wait_recv()
             total = total + contribution(zrecv[i, d], lax.rem(s + n - d, n))
+        swaps = []
         for t in range(TW):
             osend[i, t] = total[:, t * lanes:(t + 1) * lanes].astype(BF)
-        copy = send(osend.at[i], orecv.at[i], os_.at[i], or_.at[i], {"obs": 1 - c})
-        copy.wait_recv()
-        out = []
-        for t in range(TW):
+            swaps.append(send(osend.at[i, t], orecv.at[i, t], os_.at[i, t], or_.at[i, t],
+                              {"obs": 1 - c}))
+
+        def summed(t):
+            swaps[t].wait_recv()
             tile = osend[i, t].astype(F32) + orecv[i, t].astype(F32)
-            out.append([tile[r * cols:(r + 1) * cols] * spread[r] for r in range(RD)])
-        return smooth(2 * i, out, False)
-
-    def smooth(h, q, forward):
-        for t in range(TW):
+            return [tile[r * cols:(r + 1) * cols] * spread[r] for r in range(RD)]
+
+        return smooth(2 * i, summed, False)
+
+    def smooth(h, fetch, forward):
+        q = {}
+
+        def stage(t):
+            q[t] = fetch(t)
             for r in range(RD):
                 hsend[h, t, r] = q[t][r].astype(BF)
+
         edge = TW - 1 if forward else 0
         step = 1 if forward else -1
         there, here = (nxt, prev) if forward else (prev, nxt)
         sides = ((high, low, 1, RD - 1, 0), (low, high, -1, 0, 1))
         waits = []
+        stage(edge)
         for j, (to, frm, ds, row, side) in enumerate(sides):
             waits.append((both(frm, here), send(
                 hsend.at[h, edge, row], hrows.at[h, side, TW], hs.at[h, 2 + j], hr.at[h, 2 + j],
                 {"space": s + ds, "tm": k + step}, both(to, there))))
         last = (here, send(
             hsend.at[h, edge], htime.at[h], hs.at[h, 4], hr.at[h, 4], {"tm": k + step}, there))
+        for t in range(TW):
+            if t != edge:
+                stage(t)
         for j, (to, frm, ds, row, side) in enumerate(sides):
             waits.append((frm, send(
                 hsend.at[h, :, row], hrows.at[h, side, pl.ds(0, TW)], hs.at[h, j], hr.at[h, j],
@@ -171,7 +182,7 @@
         return out
 
     def correlate(h, field):
-        done = smooth(h, field, True)
+        done = smooth(h, field.__getitem__, True)
         return [[done[t][r] * spread[r] for r in range(RD)] for t in range(TW)]
 
     def observe(i, field):
@@ -269,7 +280,7 @@
                 pltpu.VMEM((4, RD, cols, members), BF),
                 pltpu.VMEM((TW, RD, cols, members), F32),
                 dma((2, n)), dma((2, n)), dma((2, n)), dma((2, n)),
-                dma((2,)), dma((2,)), dma((4, 5)), dma((4, 5)),
+                dma((2, TW)), dma((2, TW)), dma((4, 5)), dma((4, 5)),
             ],
             compiler_params=pltpu.CompilerParams(
                 collective_id=0, has_side_effects=True, vmem_limit_bytes=63 * 1024 * 1024

time: 57.9 us -> 57.7 us (level)
  no operation moved by 1% of the time
where the time goes in v5:
time: 57.7 us; the launch traced here: 57.5 us
  Pallas kernels  53.9 us (93%)
  local copies, waits for them, and re-layouts  2.36 us (4%)
  between operations  1.29 us (2%)
    pallas_call x1, Pallas kernels, shards(): pl.pallas_call(functools.partial(kernel, n, nt), out_shape=(jax.ShapeDtyp...  53.9 us
    unnamed x4, local copies, waits for them, and re-layouts  2.36 us

profile of v5, /device:TPU:0, one launch (start us, length us, event | category | flops | bytes accessed | tf_op | source)
XLA Modules:
  0.0 57.5 jit_solution(682393823921639154)
XLA Ops:
  1.3 53.9 %shard_map.104 = (f32[2,2,128,128]{3,2,1,0:T(8,128)}, f32[1,1,256,128]{3,2,1,0:T(8,128)}) custom-call(bf16[1,1,4,256,256]{4,3,2,1,0:T(8,128)(2,1)} %fp_in.1, s32[1,1,4]{2,1,0:T(1,128)} %which_in.1, s32[1,4]{1,0:T(1,128)} %order_in.1, s32[1]{0:T(128)S(6)} %copy.13.land_in, f32[2,128]{1,0:T(2,128)} %sigma_in.1, f32[1,1,256,128]{3,2,1,0:T(8,128)} %dep_in.1, ...), custom_call_target="tpu_custom_call" | custom-call | tf_op jit(solution)/shard_map/pallas_call | solution.py:253
  55.1 0.0 copy-start
  55.2 1.7 %copy.14 = f32[2,2,128,128]{3,2,1,0:T(8,128)} copy(f32[2,2,128,128]{3,2,1,0:T(8,128)} %get-tuple-element.4) | data formatting | bytes 524288
  56.9 0.0 copy-done
  56.9 0.7 %copy.15 = f32[1,1,256,128]{3,2,1,0:T(8,128)} copy(f32[1,1,256,128]{3,2,1,0:T(8,128)S(1)} %copy-done) | data formatting | bytes 262144
Async XLA Ops:
  55.1 1.7 %copy-start = (f32[1,1,256,128]{3,2,1,0:T(8,128)S(1)}, f32[1,1,256,128]{3,2,1,0:T(8,128)}, u32[]{:S(2)}) copy-start(f32[1,1,256,128]{3,2,1,0:T(8,128)} %get-tuple-element.5) | copy-start | bytes 393220
